TPU v7x, 256 devices: a whole 4x4x8 slice. The times are simulated.
256 devices in a mesh: dp: 4 (over y_lo, core), seq: 8 (over y_hi, x), head: 8 (over z).
Axes of the slice: x: 4, y: 4 (y_hi: 2, y_lo: 2; y = y_hi * 2 + y_lo), z: 8, core: 2. Of those that a mesh axis runs over, the one named last changes fastest.
Arguments:
- queries: bfloat16 [4, 2048, 3072], P('dp', 'seq', 'head'), may hold values from -160 to 160
- key_cache: bfloat16 [4, 2048, 1024], P('dp', 'seq', 'head'), may hold values from -7 to 7
- value_cache: bfloat16 [4, 2048, 1024], P('dp', 'seq', 'head'), may hold values from -6 to 6
- out_grad: bfloat16 [4, 2048, 3072], P('dp', 'seq', 'head'), may hold values from -6 to 6
- doc_ids: int32 [4, 2048], P('dp', 'seq'), may hold values from 0 to 1, never falling along the last dimension, each value on 1 to 2047 neighbouring positions
- layer_input: bfloat16 [4, 2048, 3072], P('dp', ('seq', 'head')), may hold values from -6 to 6
- key_proj: bfloat16 [3072, 1024], P(None, 'head'), may hold values from -0.109375 to 0.109375
- value_proj: bfloat16 [3072, 1024], P(None, 'head'), may hold values from -0.109375 to 0.109375
Outputs:
- query_grad: bfloat16 [4, 2048, 3072], P('dp', 'seq', 'head')
- input_grad: bfloat16 [4, 2048, 3072], P('dp', ('seq', 'head'))
- grad_keyproj: float32 [3072, 1024], P(None, 'head')
- grad_valueproj: float32 [3072, 1024], P(None, 'head')
Inputs may be any that keep to these rules, and one draw needn't show every extreme that they name: `doc_ids`: document numbers never fall along a sequence; a document spans 1 to 2047 positions.
All inputs are finite; a program needn't handle non-finite values.
Results may differ from a plain program's by a relative error of at most 0.02.
Values may be sent and summed in bfloat16 or wider, within the bound.
A program may use at most 64 MiB of HBM per device.

v0:
```python
import jax
import jax.numpy as jnp
from jax import lax
from jax.sharding import PartitionSpec as P

D = 3072
HD = 128
GROUP = 3
NEG_FILL = -1e30


def in_order(tiles, dim):
    shape = list(tiles.shape[1:])
    shape[dim] *= tiles.shape[0]
    return jnp.moveaxis(tiles, 0, dim).reshape(shape)


def sent_to_all(x, axis):
    peers = lax.axis_size(axis)
    return lax.all_to_all(jnp.broadcast_to(x[None], (peers, *x.shape)), axis, 0, 0, tiled=True)


def collect(x, axis, dim):
    return in_order(sent_to_all(x, axis), dim)


def in_blocks(x, dim, peers):
    shape = x.shape
    tiles = x.reshape(*shape[:dim], peers, shape[dim] // peers, *shape[dim + 1 :])
    return jnp.moveaxis(tiles, dim, 0)


def sum_at_owner(x, axis, dim):
    tiles = in_blocks(x, dim, lax.axis_size(axis))
    arrived = lax.all_to_all(tiles, axis, split_axis=0, concat_axis=0, tiled=True)
    return arrived.astype(jnp.float32).sum(axis=0)


def shards(queries, key_cache, value_cache, out_grad, doc_ids, layer_input, key_proj, value_proj):
    rows_query = queries.shape[1]
    col_width = key_cache.shape[2]
    kv_heads = col_width // HD
    cycle_size = lax.axis_size("seq")
    head_count = lax.axis_size("head")
    own_index = lax.axis_index("seq")
    score_scale = HD ** (-0.5)
    query_four = queries[0].reshape(rows_query, kv_heads, GROUP, HD)
    grad_four = out_grad[0].reshape(rows_query, kv_heads, GROUP, HD)
    own_blocks = jnp.stack([key_cache[0], value_cache[0]])
    all_docs = collect(doc_ids, "seq", 1)[0]
    query_doc = doc_ids[0]
    query_pos = own_index * rows_query + lax.iota(jnp.int32, rows_query)
    last_pos = own_index * rows_query + rows_query - 1

    def block_scores(kv_piece, row_start):
        row_total = kv_piece.shape[1]
        key_block = kv_piece[0].reshape(row_total, kv_heads, HD)
        value_block = kv_piece[1].reshape(row_total, kv_heads, HD)
        key_pos = row_start + lax.iota(jnp.int32, row_total)
        key_doc = lax.dynamic_slice_in_dim(all_docs, row_start, row_total)
        allowed = (key_pos[None, :] <= query_pos[:, None]) & (
            key_doc[None, :] == query_doc[:, None]
        )
        scores = (
            jnp.einsum("ihge,jhe->hgij", query_four, key_block, preferred_element_type=jnp.float32)
            * score_scale
        )
        masked = jnp.where(allowed, scores, NEG_FILL)
        weight_grad = jnp.einsum(
            "ihge,jhe->hgij", grad_four, value_block, preferred_element_type=jnp.float32
        )
        return (key_block, allowed, masked, weight_grad)

    def stats_block(state_in, kv_piece, row_start):
        row_top, row_sum, row_acc = state_in
        key_block, allowed, masked, weight_grad = block_scores(kv_piece, row_start)
        new_top = jnp.maximum(row_top, jnp.max(masked, axis=-1))
        weights = jnp.where(allowed, jnp.exp(masked - new_top[..., None]), 0.0)
        decay = jnp.exp(row_top - new_top)
        return (
            new_top,
            row_sum * decay + jnp.sum(weights, axis=-1),
            row_acc * decay + jnp.sum(weights * weight_grad, axis=-1),
        )

    def stats_fold(state_in, kv_piece, row_start):
        row_total = kv_piece.shape[1]
        sub_rows = min(row_total, rows_query)

        def one_part(part_num, state_mid):
            part_start = row_start + part_num * sub_rows
            sub_piece = kv_piece
            return lax.cond(
                part_start <= last_pos,
                lambda: stats_block(state_mid, sub_piece, part_start),
                lambda: state_mid,
            )

        return lax.fori_loop(0, row_total // sub_rows, one_part, state_in)

    stat_shape = (kv_heads, GROUP, rows_query)
    stats_init = (
        jnp.full(stat_shape, NEG_FILL, jnp.float32),
        jnp.zeros(stat_shape, jnp.float32),
        jnp.zeros(stat_shape, jnp.float32),
    )
    all_blocks = collect(own_blocks, "seq", 1)
    row_top, row_sum, row_acc = lax.fori_loop(
        0,
        cycle_size,
        lambda block_num, state_mid: stats_fold(
            state_mid,
            lax.dynamic_slice_in_dim(all_blocks, block_num * rows_query, rows_query, 1),
            block_num * rows_query,
        ),
        stats_init,
    )
    log_total = row_top + jnp.log(row_sum)
    row_delta = row_acc / row_sum

    def grad_block(kv_piece, row_start):
        row_total = kv_piece.shape[1]
        key_block, allowed, masked, weight_grad = block_scores(kv_piece, row_start)
        weights = jnp.where(allowed, jnp.exp(masked - log_total[..., None]), 0.0)
        score_grad = (weights * (weight_grad - row_delta[..., None]) * score_scale).astype(
            jnp.bfloat16
        )
        weights_low = weights.astype(jnp.bfloat16)
        query_add = jnp.einsum(
            "hgij,jhe->ihge", score_grad, key_block, preferred_element_type=jnp.float32
        )
        key_add = jnp.einsum(
            "hgij,ihge->jhe", score_grad, query_four, preferred_element_type=jnp.float32
        )
        value_add = jnp.einsum(
            "hgij,ihge->jhe", weights_low, grad_four, preferred_element_type=jnp.float32
        )
        return (
            query_add,
            jnp.stack(
                [key_add.reshape(row_total, col_width), value_add.reshape(row_total, col_width)]
            ),
        )

    zero_query = jnp.zeros((rows_query, kv_heads, GROUP, HD), jnp.float32)

    def guarded(kv_piece, row_start):
        return lax.cond(
            row_start <= last_pos,
            lambda: grad_block(kv_piece, row_start),
            lambda: (zero_query, jnp.zeros(kv_piece.shape, jnp.float32)),
        )

    def gathered_turn(block_num, state_mid):
        grad_terms, query_sum = state_mid
        row_start = block_num * rows_query
        kv_piece = lax.dynamic_slice_in_dim(all_blocks, row_start, rows_query, 1)
        query_add, kv_add = guarded(kv_piece, row_start)
        return (
            lax.dynamic_update_slice_in_dim(grad_terms, kv_add, row_start, 1),
            query_sum + query_add,
        )

    terms_init = jnp.zeros(all_blocks.shape, jnp.float32)
    grad_terms, query_sum = lax.fori_loop(0, cycle_size, gathered_turn, (terms_init, zero_query))
    kv_grads = sum_at_owner(grad_terms.astype(jnp.bfloat16), "seq", 1)
    query_grad = query_sum.astype(jnp.bfloat16).reshape(1, rows_query, kv_heads * GROUP * HD)
    kv_low = kv_grads.astype(jnp.bfloat16)
    input_rows = rows_query // head_count
    contract_cols = (((1,), (1,)), ((), ()))
    sub_grads = kv_low
    key_term = lax.dot_general(
        sub_grads[0], key_proj, contract_cols, preferred_element_type=jnp.float32
    )
    value_term = lax.dot_general(
        sub_grads[1], value_proj, contract_cols, preferred_element_type=jnp.float32
    )
    input_sum = lax.psum_scatter(
        (key_term + value_term).astype(jnp.bfloat16), "head", scatter_dimension=0, tiled=True
    )
    input_grad = input_sum.reshape(1, input_rows, D)
    contract_rows = (((0,), (0,)), ((), ()))
    input_piece = collect(layer_input[0], "head", 0)
    row_total = input_piece.shape[0]
    sub_grads = kv_low
    key_part = lax.dot_general(
        input_piece, sub_grads[0], contract_rows, preferred_element_type=jnp.float32
    )
    value_part = lax.dot_general(
        input_piece, sub_grads[1], contract_rows, preferred_element_type=jnp.float32
    )
    grad_keyproj, grad_valueproj = (
        lax.psum(key_part.astype(jnp.bfloat16), ("dp", "seq")).astype(jnp.float32),
        lax.psum(value_part.astype(jnp.bfloat16), ("dp", "seq")).astype(jnp.float32),
    )
    return (query_grad, input_grad, grad_keyproj, grad_valueproj)


def solution(mesh):
    return jax.shard_map(
        shards,
        mesh=mesh,
        in_specs=(
            P("dp", "seq", "head"),
            P("dp", "seq", "head"),
            P("dp", "seq", "head"),
            P("dp", "seq", "head"),
            P("dp", "seq"),
            P("dp", ("seq", "head"), None),
            P(None, "head"),
            P(None, "head"),
        ),
        out_specs=(
            P("dp", "seq", "head"),
            P("dp", ("seq", "head"), None),
            P(None, "head"),
            P(None, "head"),
        ),
        check_vma=False,
    )
```

profile of v0, /device:TPU:6, one launch (start us, length us, event | category | flops | bytes accessed | tf_op | source)
XLA Modules:
  0.0 297.8 jit_solution(2051672772160471777)
XLA Ops:
  9.2 22.5 %all_to_all.20 = bf16[8,2,256,128]{3,2,1,0:T(8,128)(2,1)S(1)} all-to-all(bf16[8,2,256,128]{3,2,1,0:T(8,128)(2,1)S(1)} %broadcast_in_dim.75), channel_id=1, replica_groups=mesh['dp'=4,'seq'=8,'head'=8] {'seq'}, dimensions={0} | all-to-all | bytes 2097152 | tf_op jit(solution)/shard_map/all_to_all | solution.py:20
  32.3 5.3 %all-to-all-start.1 = ((s32[8,1,256]{2,1,0:T(1,128)}), s32[8,1,256]{2,1,0:T(1,128)S(1)}, u32[]{:S(2)}, u32[]{:S(2)}) async-start(s32[8,1,256]{2,1,0:T(1,128)} %broadcast_in_dim.77), calls=%async_computation.1 | async-start | bytes 16384 | tf_op jit(solution)/shard_map/all_to_all | solution.py:20
  39.3 4.0 %all-to-all-done.1 = s32[8,1,256]{2,1,0:T(1,128)S(1)} async-done(((s32[8,1,256]{2,1,0:T(1,128)}), s32[8,1,256]{2,1,0:T(1,128)S(1)}, u32[]{:S(2)}, u32[]{:S(2)}) %all-to-all-start.1) | async-done | bytes 8224 | tf_op jit(solution)/shard_map/all_to_all | solution.py:20
  43.3 11.4 %while.49 = (s32[]{:T(128)}, f32[1,3,256]{2,1,0:T(4,128)S(1)}, f32[1,3,256]{2,1,0:T(4,128)S(1)}, f32[1,3,256]{2,1,0:T(4,128)S(1)}, s32[]{:T(128)}, /*index=5*/s3...) while((s32[]{:T(128)}, f32[1,3,256]{2,1,0:T(4,128)S(1)}, ...), condition=%wide.region_6.7_spmd.clone, body=%wide.region_0.6_spmd.clone.sunk | while | flops 102828800 | bytes 3211637 | solution.py:108
  43.3 2.8 conditional.6
  44.7 1.2 fusion.7
  46.1 2.8 conditional.6
  47.5 1.2 fusion.7
  48.9 2.8 conditional.6
  50.3 1.2 fusion.7
  51.7 2.8 conditional.6
  55.8 23.7 %while.50 = (s32[]{:T(128)}, bf16[2,2048,128]{2,1,0:T(8,128)(2,1)}, f32[256,1,3,128]{0,3,2,1:T(8,128)S(1)}, s32[]{:T(128)}, bf16[2,2048,128]{2,1,0:T(8,128)(2,1)...) while((s32[]{:T(128)}, bf16[2,2048,128]{2,1,0:T(8,128)(2,1)}, ...), condition=%wide.region_10.0_spmd.clone, body=%wide.region_7.10_spmd.clone.sunk | while | flops 253886976 | bytes 6900105 | solution.py:165
  55.8 4.2 %conditional.7 = (f32[256,1,3,128]{0,3,2,1:T(8,128)S(1)}, bf16[2,256,128]{2,1,0:T(8,128)(2,1)S(1)}) conditional(s32[]{:T(128)} %convert_element_type.80, () %tuple.114, (bf16[2,2048,128]{2,1,0:T(8,128)(2,1)}, s32[]{:T(128)}, s32[]{:T(128)}, s32[]{:T(128)}, s32[2048]{0:T(1024)S(1)}, /*index=5*/s32[1,256]{1,0:T(1,128)S(1)}, ...), branch_computations={%region_8.8_spmd, %region_9.9_spmd} | conditional | flops 253690368 | bytes 5456462 | solution.py:148
  56.0 1.2 fusion.21
  60.8 4.2 %conditional.7 = (f32[256,1,3,128]{0,3,2,1:T(8,128)S(1)}, bf16[2,256,128]{2,1,0:T(8,128)(2,1)S(1)}) conditional(s32[]{:T(128)} %convert_element_type.80, () %tuple.114, (bf16[2,2048,128]{2,1,0:T(8,128)(2,1)}, s32[]{:T(128)}, s32[]{:T(128)}, s32[]{:T(128)}, s32[2048]{0:T(1024)S(1)}, /*index=5*/s32[1,256]{1,0:T(1,128)S(1)}, ...), branch_computations={%region_8.8_spmd, %region_9.9_spmd} | conditional | flops 253690368 | bytes 5456462 | solution.py:148
  61.0 1.2 fusion.21
  65.8 4.2 %conditional.7 = (f32[256,1,3,128]{0,3,2,1:T(8,128)S(1)}, bf16[2,256,128]{2,1,0:T(8,128)(2,1)S(1)}) conditional(s32[]{:T(128)} %convert_element_type.80, () %tuple.114, (bf16[2,2048,128]{2,1,0:T(8,128)(2,1)}, s32[]{:T(128)}, s32[]{:T(128)}, s32[]{:T(128)}, s32[2048]{0:T(1024)S(1)}, /*index=5*/s32[1,256]{1,0:T(1,128)S(1)}, ...), branch_computations={%region_8.8_spmd, %region_9.9_spmd} | conditional | flops 253690368 | bytes 5456462 | solution.py:148
  66.0 1.2 fusion.21
  70.8 4.2 %conditional.7 = (f32[256,1,3,128]{0,3,2,1:T(8,128)S(1)}, bf16[2,256,128]{2,1,0:T(8,128)(2,1)S(1)}) conditional(s32[]{:T(128)} %convert_element_type.80, () %tuple.114, (bf16[2,2048,128]{2,1,0:T(8,128)(2,1)}, s32[]{:T(128)}, s32[]{:T(128)}, s32[]{:T(128)}, s32[2048]{0:T(1024)S(1)}, /*index=5*/s32[1,256]{1,0:T(1,128)S(1)}, ...), branch_computations={%region_8.8_spmd, %region_9.9_spmd} | conditional | flops 253690368 | bytes 5456462 | solution.py:148
  71.1 1.2 fusion.21
  79.4 1.3 copy.48
  80.8 44.8 %all_to_all.21 = bf16[8,2,256,128]{3,2,1,0:T(8,128)(2,1)} all-to-all(bf16[8,2,256,128]{3,2,1,0:T(8,128)(2,1)S(1)} %copy.48), channel_id=1, replica_groups=mesh['dp'=4,'seq'=8,'head'=8] {'seq'}, dimensions={0} | all-to-all | bytes 2097152 | tf_op jit(solution)/shard_map/all_to_all | solution.py:35
  125.5 1.3 broadcast_in_dim.80
  126.8 8.5 %all-to-all-start.3 = ((bf16[8,32,3072]{2,1,0:T(8,128)(2,1)}), bf16[8,32,3072]{2,1,0:T(8,128)(2,1)S(1)}, u32[]{:S(2)}, u32[]{:S(2)}) async-start(bf16[8,32,3072]{2,1,0:T(8,128)(2,1)} %broadcast_in_dim.80), calls=%async_computation.4 | async-start | bytes 3145728 | tf_op jit(solution)/shard_map/all_to_all | solution.py:20
  135.3 1.4 reduce_sum.34
  136.7 34.5 %all-to-all-done.3 = bf16[8,32,3072]{2,1,0:T(8,128)(2,1)S(1)} async-done(((bf16[8,32,3072]{2,1,0:T(8,128)(2,1)}), bf16[8,32,3072]{2,1,0:T(8,128)(2,1)S(1)}, u32[]{:S(2)}, u32[]{:S(2)}) %all-to-all-start.3) | async-done | bytes 1572896 | tf_op jit(solution)/shard_map/all_to_all | solution.py:20
  171.2 1.3 fusion.33
  172.5 1.3 fusion.34
  174.9 1.7 fusion.32
  177.5 108.8 %all-reduce.3.cloned.1.call-done = (bf16[3072,128]{0,1:T(8,128)(2,1)}, bf16[3072,128]{0,1:T(8,128)(2,1)}) async-done(((bf16[3072,128]{0,1:T(8,128)(2,1)}, bf16[3072,128]{0,1:T(8,128)(2,1)}), (bf16[3072,128]{0,1:T(8,128)(2,1)}, bf16[3072,128]{0,1:T(8,128)(2,1)})) %all-reduce.3.cloned.1.call-update) | async-done | bytes 1572880 | tf_op jit(solution)/shard_map/psum | solution.py:193
  286.4 2.6 copy.50
  289.0 1.4 copy.51
  (149 shorter events, 32.3 us)
Async XLA Ops:
  8.0 165.8 %copy-start = (bf16[3072,128]{1,0:T(8,128)(2,1)S(1)}, bf16[3072,128]{1,0:T(8,128)(2,1)}, u32[]{:S(2)}) copy-start(bf16[3072,128]{1,0:T(8,128)(2,1)} %param.22) | copy-start | bytes 2359300
  9.0 22.7 %copy-start.6 = (s32[1,256]{1,0:T(1,128)S(1)}, s32[1,256]{1,0:T(1,128)}, u32[]{:S(2)}) copy-start(s32[1,256]{1,0:T(1,128)} %param.20) | copy-start | bytes 3076
  9.0 28.6 %copy-start.4 = (bf16[1,256,384]{2,1,0:T(8,128)(2,1)S(1)}, bf16[1,256,384]{2,1,0:T(8,128)(2,1)}, u32[]{:S(2)}) copy-start(bf16[1,256,384]{2,1,0:T(8,128)(2,1)} %param.16) | copy-start | bytes 589828
  9.2 28.7 %copy-start.5 = (bf16[1,256,384]{2,1,0:T(8,128)(2,1)S(1)}, bf16[1,256,384]{2,1,0:T(8,128)(2,1)}, u32[]{:S(2)}) copy-start(bf16[1,256,384]{2,1,0:T(8,128)(2,1)} %param.19) | copy-start | bytes 589828
  32.3 10.9 %all-to-all-start.1 = ((s32[8,1,256]{2,1,0:T(1,128)}), s32[8,1,256]{2,1,0:T(1,128)S(1)}, u32[]{:S(2)}, u32[]{:S(2)}) async-start(s32[8,1,256]{2,1,0:T(1,128)} %broadcast_in_dim.77), calls=%async_computation.1 | async-start | bytes 16384 | tf_op jit(solution)/shard_map/all_to_all | solution.py:20
  80.7 44.8 %copy-start.3 = (bf16[1,32,3072]{2,1,0:T(8,128)(2,1)S(1)}, bf16[1,32,3072]{2,1,0:T(8,128)(2,1)}, u32[]{:S(2)}) copy-start(bf16[1,32,3072]{2,1,0:T(8,128)(2,1)} %param.21) | copy-start | bytes 589828
  126.8 44.3 %all-to-all-start.3 = ((bf16[8,32,3072]{2,1,0:T(8,128)(2,1)}), bf16[8,32,3072]{2,1,0:T(8,128)(2,1)S(1)}, u32[]{:S(2)}, u32[]{:S(2)}) async-start(bf16[8,32,3072]{2,1,0:T(8,128)(2,1)} %broadcast_in_dim.80), calls=%async_computation.4 | async-start | bytes 3145728 | tf_op jit(solution)/shard_map/all_to_all | solution.py:20
  135.3 151.1 %all-reduce.3.cloned.1.call-start = ((), (), s32[]{:S(2)}) async-start(), calls=%async_computation.6 | async-start | bytes 3145728 | tf_op jit(solution)/shard_map/psum | solution.py:193
  173.8 1.1 copy-start.2
  173.8 116.6 %reduce-scatter.2.cloned.1.call-start = ((), (), s32[]{:S(2)}) async-start(), calls=%async_computation.5 | async-start | bytes 1769472 | tf_op jit(solution)/shard_map/reduce_scatter | solution.py:178
  286.4 2.6 copy-start.1
Sparse Core Ops, SparseCore 0:
  173.9 112.4 all-reduce.2
Sparse Core Ops, SparseCore 1:
  177.4 34.9 reduce-scatter.1
where the time goes:
time: 300 us; the launch traced here: 298 us
  waiting for transfers between devices  147 us (49%)
  blocking collectives  67.3 us (22%)
  matrix products  29.5 us (10%)
  local copies, waits for them, and re-layouts  17.7 us (6%)
  between operations  15.6 us (5%)
  starting transfers between devices  13.8 us (5%)
  other arithmetic  5.27 us (2%)
    psum x1, waiting for transfers between devices, shards(): lax.psum(key_part.astype(jnp.bfloat16), ('dp', 'seq')).astype(jnp.float32)  109 us
    all_to_all x1, blocking collectives, sum_at_owner(): lax.all_to_all(tiles, axis, split_axis=0, concat_axis=0, tiled=True)  44.8 us
    all_to_all x2, waiting for transfers between devices, sent_to_all(): lax.all_to_all(jnp.broadcast_to(x[None], (peers, *x.shape)), axis, 0, 0,...  38.4 us
    all_to_all x1, blocking collectives, sent_to_all(): lax.all_to_all(jnp.broadcast_to(x[None], (peers, *x.shape)), axis, 0, 0,...  22.5 us
    all_to_all x2, starting transfers between devices, sent_to_all(): lax.all_to_all(jnp.broadcast_to(x[None], (peers, *x.shape)), axis, 0, 0,...  13.8 us
    dot_general x8, matrix products, block_scores(): jnp.einsum('ihge,jhe->hgij', query_four, key_block, preferred_element_typ...  9.29 us
    dot_general x8, matrix products, block_scores(): jnp.einsum('ihge,jhe->hgij', grad_four, value_block, preferred_element_ty...  9.06 us
  transfers between devices with their start and end apart: 4, of which 3 were waited for; matrix products, arithmetic and copies ran while one was open for 3% of the time, Pallas kernels for 0%

commit v1 on v0

--- a/solution.py
+++ b/solution.py
@@ -37,6 +37,10 @@
 
 
 def shards(queries, key_cache, value_cache, out_grad, doc_ids, layer_input, key_proj, value_proj):
+
+    def lift_block(chunk, axis_id):
+        return lax.all_gather(chunk, axis_name=axis_id).sum(axis=0)
+
     rows_query = queries.shape[1]
     col_width = key_cache.shape[2]
     kv_heads = col_width // HD
@@ -190,7 +194,7 @@
         input_piece, sub_grads[1], contract_rows, preferred_element_type=jnp.float32
     )
     grad_keyproj, grad_valueproj = (
-        lax.psum(key_part.astype(jnp.bfloat16), ("dp", "seq")).astype(jnp.float32),
+        lift_block(key_part.astype(jnp.bfloat16), axis_id=("dp", "seq")).astype(jnp.float32),
         lax.psum(value_part.astype(jnp.bfloat16), ("dp", "seq")).astype(jnp.float32),
     )
     return (query_grad, input_grad, grad_keyproj, grad_valueproj)

time: 300 us -> 467 us (1.56)
  waiting for transfers between devices: 147 us -> 287 us
  local copies, waits for them, and re-layouts: 17.7 us -> 33 us
  other arithmetic: 5.27 us -> 14.5 us
    all_gather x0 -> x1, waiting for transfers between devices: none -> 144 us  [lift_block(): return lax.all_gather(chunk, axis_name=axis_id).sum(axis=0)]
    unnamed x21 -> x22, local copies, waits for them, and re-layouts: 5.99 us -> 28.7 us
    reduce_sum x0 -> x1, other arithmetic: none -> 9.23 us  [lift_block(): return lax.all_gather(chunk, axis_name=axis_id).sum(axis=0)]
    dynamic_update_slice x8, local copies, waits for them, and re-layouts: 5.37 us -> 0.21 us  [gathered_turn(): lax.dynamic_update_slice_in_dim(grad_terms, kv_add, row_start, 1)]
  transfers between devices with their start and end apart: 4 -> 5, of which waited for: 3 -> 4; matrix products, arithmetic and copies ran while one was open for 3% -> 9% of each run, Pallas kernels for 0% -> 0%
where the time goes in v1:
time: 467 us; the launch traced here: 463 us
  waiting for transfers between devices  287 us (61%)
  blocking collectives  67.4 us (14%)
  local copies, waits for them, and re-layouts  33 us (7%)
  matrix products  29.6 us (6%)
  between operations  15.7 us (3%)
  other arithmetic  14.5 us (3%)
  starting transfers between devices  13.9 us (3%)
    all_gather x1, waiting for transfers between devices, lift_block(): return lax.all_gather(chunk, axis_name=axis_id).sum(axis=0)  144 us
    psum x1, waiting for transfers between devices, shards(): lax.psum(value_part.astype(jnp.bfloat16), ('dp', 'seq')).astype(jnp.float32)  105 us
    all_to_all x1, blocking collectives, sum_at_owner(): lax.all_to_all(tiles, axis, split_axis=0, concat_axis=0, tiled=True)  44.9 us
    all_to_all x2, waiting for transfers between devices, sent_to_all(): lax.all_to_all(jnp.broadcast_to(x[None], (peers, *x.shape)), axis, 0, 0,...  38.4 us
    unnamed x22, local copies, waits for them, and re-layouts  28.7 us
    all_to_all x1, blocking collectives, sent_to_all(): lax.all_to_all(jnp.broadcast_to(x[None], (peers, *x.shape)), axis, 0, 0,...  22.5 us
    all_to_all x2, starting transfers between devices, sent_to_all(): lax.all_to_all(jnp.broadcast_to(x[None], (peers, *x.shape)), axis, 0, 0,...  13.7 us
  transfers between devices with their start and end apart: 5, of which 4 were waited for; matrix products, arithmetic and copies ran while one was open for 9% of the time, Pallas kernels for 0%

profile of v1, /device:TPU:6, one launch (start us, length us, event | category | flops | bytes accessed | tf_op | source)
XLA Modules:
  0.0 463.1 jit_solution(11708358642509857053)
XLA Ops:
  9.2 22.5 %all_to_all.20 = bf16[8,2,256,128]{3,2,1,0:T(8,128)(2,1)S(1)} all-to-all(bf16[8,2,256,128]{3,2,1,0:T(8,128)(2,1)S(1)} %broadcast_in_dim.75), channel_id=1, replica_groups=mesh['dp'=4,'seq'=8,'head'=8] {'seq'}, dimensions={0} | all-to-all | bytes 2097152 | tf_op jit(solution)/shard_map/all_to_all | solution.py:20
  32.3 5.3 %all-to-all-start.1 = ((s32[8,1,256]{2,1,0:T(1,128)}), s32[8,1,256]{2,1,0:T(1,128)S(1)}, u32[]{:S(2)}, u32[]{:S(2)}) async-start(s32[8,1,256]{2,1,0:T(1,128)} %broadcast_in_dim.77), calls=%async_computation.1 | async-start | bytes 16384 | tf_op jit(solution)/shard_map/all_to_all | solution.py:20
  39.3 4.0 all-to-all-done.1
  43.3 11.5 %while.49 = (s32[]{:T(128)}, f32[1,3,256]{2,1,0:T(4,128)S(1)}, f32[1,3,256]{2,1,0:T(4,128)S(1)}, f32[1,3,256]{2,1,0:T(4,128)S(1)}, s32[]{:T(128)}, /*index=5*/s3...) while((s32[]{:T(128)}, f32[1,3,256]{2,1,0:T(4,128)S(1)}, ...), condition=%wide.region_6.7_spmd.clone, body=%wide.region_0.6_spmd.clone.sunk | while | flops 102828800 | bytes 3211629 | solution.py:112
  43.3 2.8 conditional.6
  44.7 1.2 fusion.7
  46.1 2.8 conditional.6
  48.9 2.8 conditional.6
  51.7 2.8 conditional.6
  54.8 18.8 %while.50 = (s32[]{:T(128)}, bf16[2,2048,128]{2,1,0:T(8,128)(2,1)S(1)}, f32[256,1,3,128]{0,3,2,1:T(8,128)S(1)}, s32[]{:T(128)}, bf16[2,2048,128]{2,1,0:T(8,128)(...) while((s32[]{:T(128)}, ...), condition=%wide.region_10.0_spmd.clone, body=%wide.region_7.10_spmd.clone.sunk | while | flops 253886976 | bytes 6899597 | solution.py:169
  54.9 4.2 conditional.7
  55.1 1.2 fusion.21
  59.3 4.2 conditional.7
  59.6 1.2 fusion.21
  63.7 4.2 conditional.7
  64.0 1.2 fusion.21
  68.1 4.2 conditional.7
  68.4 1.2 fusion.21
  73.7 44.9 %all_to_all.21 = bf16[8,2,256,128]{3,2,1,0:T(8,128)(2,1)} all-to-all(bf16[8,2,256,128]{3,2,1,0:T(8,128)(2,1)S(1)} %copy.46), channel_id=1, replica_groups=mesh['dp'=4,'seq'=8,'head'=8] {'seq'}, dimensions={0} | all-to-all | bytes 2097152 | tf_op jit(solution)/shard_map/all_to_all | solution.py:35
  118.6 1.3 broadcast_in_dim.80
  119.9 8.5 %all-to-all-start.3 = ((bf16[8,32,3072]{2,1,0:T(8,128)(2,1)}), bf16[8,32,3072]{2,1,0:T(8,128)(2,1)S(1)}, u32[]{:S(2)}, u32[]{:S(2)}) async-start(bf16[8,32,3072]{2,1,0:T(8,128)(2,1)} %broadcast_in_dim.80), calls=%async_computation.4 | async-start | bytes 3145728 | tf_op jit(solution)/shard_map/all_to_all | solution.py:20
  128.4 1.4 reduce_sum.46
  129.8 34.4 %all-to-all-done.3 = bf16[8,32,3072]{2,1,0:T(8,128)(2,1)S(1)} async-done(((bf16[8,32,3072]{2,1,0:T(8,128)(2,1)}), bf16[8,32,3072]{2,1,0:T(8,128)(2,1)S(1)}, u32[]{:S(2)}, u32[]{:S(2)}) %all-to-all-start.3) | async-done | bytes 1572896 | tf_op jit(solution)/shard_map/all_to_all | solution.py:20
  164.2 1.3 fusion.34
  165.6 1.3 fusion.33
  168.0 1.8 fusion.32
  170.7 105.3 %all-reduce.2.cloned.1.call-done = bf16[3072,128]{0,1:T(8,128)(2,1)} async-done(((bf16[3072,128]{0,1:T(8,128)(2,1)}), bf16[3072,128]{0,1:T(8,128)(2,1)}) %all-reduce.2.cloned.1.call-update) | async-done | bytes 786448 | tf_op jit(solution)/shard_map/psum | solution.py:198
  276.0 2.5 copy.49
  278.5 143.7 %all-gather.3.cloned.1.call-done = bf16[98304,128]{0,1:T(8,128)(2,1)} async-done(((bf16[3072,128]{0,1:T(8,128)(2,1)}), bf16[98304,128]{0,1:T(8,128)(2,1)}) %all-gather.3.cloned.1.call-update) | async-done | bytes 25165840 | tf_op jit(solution)/shard_map/all_gather | solution.py:42
  422.3 22.7 %copy.53 = bf16[16,8,32,3072]{3,2,1,0:T(8,128)(2,1)S(1)} copy(bf16[16,8,32,3072]{3,1,2,0:T(8,128)(2,1)} %bitcast.156) | data formatting | bytes 50331648
  445.0 9.2 %bitcast_reduce_fusion = bf16[3072,128]{0,1:T(8,128)(2,1)S(1)} fusion(bf16[16,8,32,3072]{3,2,1,0:T(8,128)(2,1)S(1)} %copy.53), kind=kLoop, calls=%fused_computation.55 | loop fusion | flops 12189696 | bytes 25952256 | tf_op jit(solution)/shard_map/reduce_sum | solution.py:42
  454.3 1.4 copy.48
  (154 shorter events, 28.8 us)
Async XLA Ops:
  8.0 159.0 %copy-start = (bf16[3072,128]{1,0:T(8,128)(2,1)S(1)}, bf16[3072,128]{1,0:T(8,128)(2,1)}, u32[]{:S(2)}) copy-start(bf16[3072,128]{1,0:T(8,128)(2,1)} %param.22) | copy-start | bytes 2359300
  9.0 22.7 %copy-start.6 = (s32[1,256]{1,0:T(1,128)S(1)}, s32[1,256]{1,0:T(1,128)}, u32[]{:S(2)}) copy-start(s32[1,256]{1,0:T(1,128)} %param.20) | copy-start | bytes 3076
  9.0 28.6 %copy-start.4 = (bf16[1,256,384]{2,1,0:T(8,128)(2,1)S(1)}, bf16[1,256,384]{2,1,0:T(8,128)(2,1)}, u32[]{:S(2)}) copy-start(bf16[1,256,384]{2,1,0:T(8,128)(2,1)} %param.16) | copy-start | bytes 589828
  9.2 28.7 %copy-start.5 = (bf16[1,256,384]{2,1,0:T(8,128)(2,1)S(1)}, bf16[1,256,384]{2,1,0:T(8,128)(2,1)}, u32[]{:S(2)}) copy-start(bf16[1,256,384]{2,1,0:T(8,128)(2,1)} %param.19) | copy-start | bytes 589828
  32.3 10.9 %all-to-all-start.1 = ((s32[8,1,256]{2,1,0:T(1,128)}), s32[8,1,256]{2,1,0:T(1,128)S(1)}, u32[]{:S(2)}, u32[]{:S(2)}) async-start(s32[8,1,256]{2,1,0:T(1,128)} %broadcast_in_dim.77), calls=%async_computation.1 | async-start | bytes 16384 | tf_op jit(solution)/shard_map/all_to_all | solution.py:20
  73.7 44.9 %copy-start.3 = (bf16[1,32,3072]{2,1,0:T(8,128)(2,1)S(1)}, bf16[1,32,3072]{2,1,0:T(8,128)(2,1)}, u32[]{:S(2)}) copy-start(bf16[1,32,3072]{2,1,0:T(8,128)(2,1)} %param.21) | copy-start | bytes 589828
  119.9 44.3 %all-to-all-start.3 = ((bf16[8,32,3072]{2,1,0:T(8,128)(2,1)}), bf16[8,32,3072]{2,1,0:T(8,128)(2,1)S(1)}, u32[]{:S(2)}, u32[]{:S(2)}) async-start(bf16[8,32,3072]{2,1,0:T(8,128)(2,1)} %broadcast_in_dim.80), calls=%async_computation.4 | async-start | bytes 3145728 | tf_op jit(solution)/shard_map/all_to_all | solution.py:20
  128.4 147.6 %all-reduce.2.cloned.1.call-start = ((), (), s32[]{:S(2)}) async-start(), calls=%async_computation.6 | async-start | bytes 1572864 | tf_op jit(solution)/shard_map/psum | solution.py:198
  165.5 256.7 %all-gather.3.cloned.1.call-start = ((), (), s32[]{:S(2)}) async-start(), calls=%async_computation.7 | async-start | bytes 25952256 | tf_op jit(solution)/shard_map/all_gather | solution.py:42
  166.9 1.1 copy-start.2
  166.9 288.8 %reduce-scatter.2.cloned.1.call-start = ((), (), s32[]{:S(2)}) async-start(), calls=%async_computation.5 | async-start | bytes 1769472 | tf_op jit(solution)/shard_map/reduce_scatter | solution.py:182
  445.0 10.7 %copy-start.1 = (bf16[3072,128]{1,0:T(8,128)(2,1)S(1)}, bf16[3072,128]{1,0:T(8,128)(2,1)}, u32[]{:S(2)}) copy-start(bf16[3072,128]{1,0:T(8,128)(2,1)} %param.22) | copy-start | bytes 2359300
Sparse Core Ops, SparseCore 0:
  165.7 110.2 all-reduce.1
  278.4 143.8 all-gather.2
Sparse Core Ops, SparseCore 1:
  170.5 34.6 reduce-scatter.1
